TPU v7x, 32 devices: a whole 2x2x4 slice. The times are simulated.
32 devices in a mesh: events: 4 (over z), nodes: 8 (over y, x, core).
Axes of the slice: x: 2, y: 2, z: 4, core: 2. Of those that a mesh axis runs over, the one named last changes fastest.
Arguments:
- nodes_in: bfloat16 [4, 16384, 128], P('events', 'nodes'), may hold values from -6 to 6
- edge_latents: bfloat16 [4, 8, 8, 2, 128, 128], P('events', 'nodes'), may hold values from -6 to 6
- src_block: int32 [4, 8, 8, 2], P('events', 'nodes'), may hold values from 0 to 15
- src_offset: int32 [4, 8, 8, 2, 128], P('events', 'nodes'), may hold values from 0 to 127
- dst_block: int32 [4, 8, 8, 2], P('events', 'nodes'), may hold values from 0 to 15
- dst_offset: int32 [4, 8, 8, 2, 128], P('events', 'nodes'), may hold values from 0 to 127
- tile_counts: int32 [4, 8, 8], P('events'), may hold values from 1 to 2, as said below
- w_edge1: bfloat16 [384, 128], replicated, may hold values from -0.3125 to 0.3125
- b_edge1: float32 [128], replicated, may hold values from -3 to 3
- w_edge2: bfloat16 [128, 128], replicated, may hold values from -0.5 to 0.5
- b_edge2: float32 [128], replicated, may hold values from -3 to 3
- w_node1: bfloat16 [256, 128], replicated, may hold values from -0.375 to 0.375
- b_node1: float32 [128], replicated, may hold values from -3 to 3
- w_node2: bfloat16 [128, 128], replicated, may hold values from -0.5 to 0.5
- b_node2: float32 [128], replicated, may hold values from -3 to 3
- cotangent: bfloat16 [4, 16384, 128], P('events', 'nodes'), may hold values from -6 to 6
Outputs:
- new_nodes: bfloat16 [4, 16384, 128], P('events', 'nodes')
- node_grads: bfloat16 [4, 16384, 128], P('events', 'nodes')
- grad_w_edge1: float32 [384, 128], replicated
- grad_b_edge1: float32 [128], replicated
- grad_w_edge2: float32 [128, 128], replicated
- grad_b_edge2: float32 [128], replicated
- grad_w_node1: float32 [256, 128], replicated
- grad_b_node1: float32 [128], replicated
- grad_w_node2: float32 [128, 128], replicated
- grad_b_node2: float32 [128], replicated
Inputs may be any that keep to these rules, and one draw needn't show every extreme that they name: tile_counts[g, s, d] is the number of live slots from source device s to destination device d; in every event group some destination device receives exactly 2 tiles from every source device.
All inputs are finite; a program needn't handle non-finite values.
Results may differ from a plain program's by a relative error of at most 0.0067.
Values may be sent and summed in bfloat16 or wider, within the bound.
A program may use at most 64 MiB of HBM per device.

v0:
```python
import jax
import jax.numpy as jnp
from jax import lax
from jax.sharding import PartitionSpec as P


def silu_slope(value):
    sig = jax.nn.sigmoid(value)
    return sig * (1.0 + value * (1.0 - sig))


def tile_onehot(offsets, tile):
    return (offsets[..., None] == jnp.arange(tile, dtype=jnp.int32)[None, None, :]).astype(
        jnp.bfloat16
    )


def gather_tiles(table, blocks, onehot):
    tile = onehot.shape[-1]
    picked = table.reshape(-1, tile, table.shape[-1])[blocks]
    return jnp.einsum("ten,tnd->ted", onehot, picked, preferred_element_type=jnp.float32).astype(
        table.dtype
    )


def scatter_tiles(values, blocks, onehot, block_count):
    if values.dtype == jnp.bfloat16:
        per_tile = jnp.einsum("ten,ted->tnd", onehot, values, preferred_element_type=jnp.float32)
    else:
        per_tile = jnp.einsum(
            "ten,ted->tnd", onehot.astype(jnp.float32), values, precision=lax.Precision.HIGHEST
        )
    picker = (blocks[:, None] == jnp.arange(block_count, dtype=jnp.int32)[None, :]).astype(
        jnp.float32
    )
    summed = jnp.einsum("tb,tnd->bnd", picker, per_tile, precision=lax.Precision.HIGHEST)
    return summed.reshape(-1, values.shape[-1])


def shards(
    nodes_in,
    edge_latents,
    src_block,
    src_offset,
    dst_block,
    dst_offset,
    tile_counts,
    w_edge1,
    b_edge1,
    w_edge2,
    b_edge2,
    w_node1,
    b_node1,
    w_node2,
    b_node2,
    cotangent,
):
    peers = lax.axis_size("nodes")
    myself = lax.axis_index("nodes")
    nodes = nodes_in[0]
    cot = cotangent[0]
    node_rows, width = nodes.shape
    tile = src_offset.shape[-1]
    slots = src_offset.shape[3]
    block_count = node_rows // tile
    tiles_all = peers * slots
    scale_factor = float(lax.axis_size("events") * peers * node_rows) ** (-0.5)
    w_src, w_dst, w_lat = (w_edge1[:width], w_edge1[width : 2 * width], w_edge1[2 * width :])
    w_own, w_agg = (w_node1[:width], w_node1[width:])
    send_blocks = src_block[0, 0].reshape(-1)
    send_hot = tile_onehot(src_offset[0, 0].reshape(tiles_all, tile), tile)
    recv_blocks = dst_block[0, 0].reshape(-1)
    recv_hot = tile_onehot(dst_offset[0, 0].reshape(tiles_all, tile), tile)
    outgoing = gather_tiles(nodes, send_blocks, send_hot).reshape(peers, slots, tile, width)
    h_src = lax.all_to_all(outgoing, "nodes", split_axis=0, concat_axis=0, tiled=True).reshape(
        -1, width
    )
    counts = lax.dynamic_index_in_dim(tile_counts[0], myself, 1, keepdims=False)
    live = jnp.arange(slots, dtype=jnp.int32)[None, :] < counts[:, None]
    live = (
        jnp.broadcast_to(live[..., None], (peers, slots, tile)).reshape(-1, 1).astype(jnp.bfloat16)
    )
    lat = edge_latents[0, 0].reshape(-1, width)
    h_dst = gather_tiles(nodes, recv_blocks, recv_hot).reshape(-1, width)
    z_one = (
        jnp.dot(h_src, w_src, preferred_element_type=jnp.float32)
        + jnp.dot(h_dst, w_dst, preferred_element_type=jnp.float32)
        + jnp.dot(lat, w_lat, preferred_element_type=jnp.float32)
        + b_edge1
    )
    a_one = jax.nn.silu(z_one).astype(jnp.bfloat16)
    message = (jnp.dot(a_one, w_edge2, preferred_element_type=jnp.float32) + b_edge2).astype(
        jnp.bfloat16
    ) * live
    agg = scatter_tiles(
        message.reshape(tiles_all, tile, width), recv_blocks, recv_hot, block_count
    ).astype(jnp.bfloat16)
    z_two = (
        jnp.dot(nodes, w_own, preferred_element_type=jnp.float32)
        + jnp.dot(agg, w_agg, preferred_element_type=jnp.float32)
        + b_node1
    )
    a_two = jax.nn.silu(z_two).astype(jnp.bfloat16)
    updated = (
        nodes.astype(jnp.float32)
        + jnp.dot(a_two, w_node2, preferred_element_type=jnp.float32)
        + b_node2
    ).astype(jnp.bfloat16)
    g_two = (
        jnp.dot(cot, w_node2.T, preferred_element_type=jnp.float32) * silu_slope(z_two)
    ).astype(jnp.bfloat16)
    node_terms = (
        jnp.concatenate(
            [
                jnp.dot(nodes.T, g_two, preferred_element_type=jnp.float32),
                jnp.dot(agg.T, g_two, preferred_element_type=jnp.float32),
            ],
            axis=0,
        ),
        jnp.sum(g_two.astype(jnp.float32), axis=0),
        jnp.dot(a_two.T, cot, preferred_element_type=jnp.float32),
        jnp.sum(cot.astype(jnp.float32), axis=0),
    )
    g_agg = jnp.dot(g_two, w_agg.T, preferred_element_type=jnp.float32).astype(jnp.bfloat16)
    g_msg = gather_tiles(g_agg, recv_blocks, recv_hot).reshape(-1, width) * live
    g_one = (
        jnp.dot(g_msg, w_edge2.T, preferred_element_type=jnp.float32) * silu_slope(z_one)
    ).astype(jnp.bfloat16)
    g_src = jnp.dot(g_one, w_src.T, preferred_element_type=jnp.float32).reshape(
        peers, slots, tile, width
    )
    returned = (
        lax.all_to_all(g_src.astype(jnp.bfloat16), "nodes", split_axis=0, concat_axis=0, tiled=True)
        .astype(g_src.dtype)
        .reshape(-1, width)
    )
    g_dst = jnp.dot(g_one, w_dst.T, preferred_element_type=jnp.float32)
    total = cot.astype(jnp.float32) + jnp.dot(g_two, w_own.T, preferred_element_type=jnp.float32)
    total = total + scatter_tiles(
        g_dst.reshape(tiles_all, tile, width), recv_blocks, recv_hot, block_count
    )
    total = total + scatter_tiles(
        returned.reshape(tiles_all, tile, width), send_blocks, send_hot, block_count
    )
    edge_terms = (
        jnp.concatenate(
            [
                jnp.dot(h_src.T, g_one, preferred_element_type=jnp.float32),
                jnp.dot(h_dst.T, g_one, preferred_element_type=jnp.float32),
                jnp.dot(lat.T, g_one, preferred_element_type=jnp.float32),
            ],
            axis=0,
        ),
        jnp.sum(g_one.astype(jnp.float32), axis=0),
        jnp.dot(a_one.T, g_msg, preferred_element_type=jnp.float32),
        jnp.sum(g_msg.astype(jnp.float32), axis=0),
    )
    summed = lax.psum(
        (
            edge_terms[0],
            edge_terms[1],
            edge_terms[2],
            edge_terms[3],
            node_terms[0],
            node_terms[1],
            node_terms[2],
            node_terms[3],
        ),
        ("events", "nodes"),
    )
    scaled = [value * scale_factor for value in summed]
    return (
        updated[None],
        total.astype(jnp.bfloat16)[None],
        scaled[0],
        scaled[1],
        scaled[2],
        scaled[3],
        scaled[4],
        scaled[5],
        scaled[6],
        scaled[7],
    )


def solution(mesh):
    return jax.shard_map(
        shards,
        mesh=mesh,
        in_specs=(
            P("events", "nodes", None),
            P("events", "nodes", None, None, None, None),
            P("events", "nodes", None, None),
            P("events", "nodes", None, None, None),
            P("events", "nodes", None, None),
            P("events", "nodes", None, None, None),
            P("events", None, None),
            P(),
            P(),
            P(),
            P(),
            P(),
            P(),
            P(),
            P(),
            P("events", "nodes", None),
        ),
        out_specs=(
            P("events", "nodes", None),
            P("events", "nodes", None),
            P(),
            P(),
            P(),
            P(),
            P(),
            P(),
            P(),
            P(),
        ),
        check_vma=False,
    )
```

profile of v0, /device:TPU:1, one launch (start us, length us, event | category | flops | bytes accessed | tf_op | source)
XLA Modules:
  0.0 243.8 jit_solution(3081769146235548526)
XLA Ops:
  8.1 1.7 gather_fusion
  9.8 1.3 convolution_convert_fusion.4
  11.1 5.4 %all-to-all-start = ((bf16[8,2,128,128]{3,2,1,0:T(8,128)(2,1)}), bf16[8,2,128,128]{3,2,1,0:T(8,128)(2,1)S(1)}, u32[]{:S(2)}, u32[]{:S(2)}) async-start(bf16[8,2,128,128]{3,2,1,0:T(8,128)(2,1)} %bitcast.6), calls=%async_computation | async-start | bytes 1048576 | tf_op jit(solution)/shard_map/all_to_all | solution.py:75
  20.9 1.2 fusion.25
  24.4 1.4 multiply_convert_fusion.1
  28.0 1.2 convolution_convert_fusion.5
  30.0 1.3 multiply_convert_fusion
  31.3 1.0 convert_reduce_fusion.1
  33.0 1.1 convolution_convert_fusion.1
  34.1 2.5 %gather_fusion.2 = bf16[16,128,128]{2,1,0:T(8,128)(2,1)} fusion(bf16[16,128,128]{2,1,0:T(8,128)(2,1)} %bitcast.107, s32[1024]{0:T(1024)S(1)} %pad_clamp_fusion), kind=kCustom, calls=%fused_computation.2 | custom fusion | bytes 1048640 | tf_op jit(solution)/shard_map/gather | solution.py:20
  36.5 2.3 convert_reduce_fusion.2
  40.8 1.0 convert_reduce_fusion.3
  43.4 1.1 convolution_convert_fusion
  46.5 1.1 fusion.11
  47.6 7.0 %all-to-all-start.1 = ((bf16[8,2,128,128]{3,2,1,0:T(8,128)(2,1)}), bf16[8,2,128,128]{3,2,1,0:T(8,128)(2,1)}, u32[]{:S(2)}, u32[]{:S(2)}) async-start(bf16[8,2,128,128]{3,2,1,0:T(8,128)(2,1)} %bitcast.104), calls=%async_computation.1 | async-start | bytes 1048576 | tf_op jit(solution)/shard_map/all_to_all | solution.py:133
  54.6 1.5 fusion.19
  56.2 2.2 fusion.15
  60.4 39.4 %all-reduce = (f32[128]{0:T(128)S(1)}, f32[128]{0:T(128)S(1)}, f32[128]{0:T(128)S(1)}, f32[128]{0:T(128)S(1)}) all-reduce(f32[128]{0:T(128)S(1)} %copy-done.26, f32[128]{0:T(128)S(1)} %copy-done.25, f32[128]{0:T(128)S(1)} %copy-done.24, f32[128]{0:T(128)S(1)} %copy-done.21), channel_id=1, replica_groups=mesh['events'=4,'nodes'=8] {'events','nodes'}, use_global_device_ids=true, to_apply=%region_2.3 | all-reduce | flops 512 | bytes 4096 | tf_op jit(solution)/shard_map/psum | solution.py:158
  100.4 1.6 copy.36
  102.5 126.7 %all-reduce.4.cloned.1.call-done = (f32[384,128]{1,0:T(8,128)}, f32[128,128]{1,0:T(8,128)}, f32[256,128]{1,0:T(8,128)}, f32[128,128]{1,0:T(8,128)}) async-done(((f32[384,128]{1,0:T(8,128)}, f32[128,128]{1,0:T(8,128)}, f32[256,128]{1,0:T(8,128)}, f32[128,128]{1,0:T(8,128)}), (f32[384,128]{1,0:T(8,128)}, f32[128,128]{1,0:T(8,128)}, f32[256,128]{1,0:T(8,128)}, ...) | async-done | bytes 458768 | tf_op jit(solution)/shard_map/psum | solution.py:158
  229.2 1.6 broadcast_multiply_fusion.1
  232.5 1.8 fusion.18
  234.2 1.2 fusion.13
  235.8 1.1 fusion.10
  (106 shorter events, 21.8 us)
Async XLA Ops:
  7.2 16.6 %copy-start = (bf16[1,1,8,2,128,128]{5,4,3,2,1,0:T(8,128)(2,1)S(1)}, bf16[1,1,8,2,128,128]{5,4,3,2,1,0:T(8,128)(2,1)}, u32[]{:S(2)}) copy-start(bf16[1,1,8,2,128,128]{5,4,3,2,1,0:T(8,128)(2,1)} %param.17) | copy-start | bytes 1572868
  8.1 1.7 copy-start.14
  11.1 6.2 %copy-start.1 = (bf16[1,2048,128]{2,1,0:T(8,128)(2,1)S(1)}, bf16[1,2048,128]{2,1,0:T(8,128)(2,1)}, u32[]{:S(2)}) copy-start(bf16[1,2048,128]{2,1,0:T(8,128)(2,1)} %param.16) | copy-start | bytes 1572868
  11.1 12.1 %all-to-all-start = ((bf16[8,2,128,128]{3,2,1,0:T(8,128)(2,1)}), bf16[8,2,128,128]{3,2,1,0:T(8,128)(2,1)S(1)}, u32[]{:S(2)}, u32[]{:S(2)}) async-start(bf16[8,2,128,128]{3,2,1,0:T(8,128)(2,1)} %bitcast.6), calls=%async_computation | async-start | bytes 1048576 | tf_op jit(solution)/shard_map/all_to_all | solution.py:75
  18.7 1.4 copy-start.2
  20.0 8.0 %copy-start.17 = (s32[16]{0:T(128)}, s32[16]{0:T(128)S(1)}, u32[]{:S(2)}) copy-start(s32[16]{0:T(128)S(1)} %eq.32) | copy-start | bytes 196
  20.9 2.2 copy-start.8
  24.4 1.5 copy-start.27
  25.8 1.1 copy-start.5
  28.0 1.4 copy-start.4
  30.0 1.3 copy-start.15
  38.8 1.0 copy-start.6
  38.8 2.0 copy-start.31
  42.5 0.9 copy-start.9
  44.5 1.0 copy-start.3
  45.5 1.0 copy-start.16
  45.5 1.0 copy-start.23
  47.6 184.8 %all-to-all-start.1 = ((bf16[8,2,128,128]{3,2,1,0:T(8,128)(2,1)}), bf16[8,2,128,128]{3,2,1,0:T(8,128)(2,1)}, u32[]{:S(2)}, u32[]{:S(2)}) async-start(bf16[8,2,128,128]{3,2,1,0:T(8,128)(2,1)} %bitcast.104), calls=%async_computation.1 | async-start | bytes 1048576 | tf_op jit(solution)/shard_map/all_to_all | solution.py:133
  54.6 174.6 %all-reduce.4.cloned.1.call-start = ((), (), s32[]{:S(2)}) async-start(), calls=%async_computation.2 | async-start | bytes 917504 | tf_op jit(solution)/shard_map/psum | solution.py:158
  54.6 1.5 copy-start.18
  229.2 1.6 copy-start.12
  229.2 1.6 copy-start.13
  230.8 1.0 copy-start.7
  232.4 1.8 copy-start.20
  (11 other events, 7.7 us)
Sparse Core Ops, SparseCore 0:
  100.0 129.1 all-reduce.3
where the time goes:
time: 245 us; the launch traced here: 244 us
  waiting for transfers between devices  128 us (52%)
  blocking collectives  39.4 us (16%)
  matrix products  28.1 us (11%)
  local copies, waits for them, and re-layouts  15.2 us (6%)
  between operations  14.3 us (6%)
  starting transfers between devices  12.4 us (5%)
  other arithmetic  6.65 us (3%)
    psum x1, waiting for transfers between devices, shards(): lax.psum((edge_terms[0], edge_terms[1], edge_terms[2], edge_terms[3], nod...  127 us
    psum x1, blocking collectives, shards(): lax.psum((edge_terms[0], edge_terms[1], edge_terms[2], edge_terms[3], nod...  39.4 us
    unnamed x66, local copies, waits for them, and re-layouts  7.1 us
    all_to_all x1, starting transfers between devices, shards(): lax.all_to_all(g_src.astype(jnp.bfloat16), 'nodes', split_axis=0, concat_...  7.01 us
    all_to_all x1, starting transfers between devices, shards(): lax.all_to_all(outgoing, 'nodes', split_axis=0, concat_axis=0, tiled=True)  5.35 us
  transfers between devices with their start and end apart: 3, of which 2 were waited for; matrix products, arithmetic and copies ran while one was open for 6% of the time, Pallas kernels for 0%

commit v1 on v0

--- a/solution.py
+++ b/solution.py
@@ -155,7 +155,7 @@
         jnp.dot(a_one.T, g_msg, preferred_element_type=jnp.float32),
         jnp.sum(g_msg.astype(jnp.float32), axis=0),
     )
-    summed = lax.psum(
+    half = lax.psum(
         (
             edge_terms[0],
             edge_terms[1],
@@ -166,8 +166,9 @@
             node_terms[2],
             node_terms[3],
         ),
-        ("events", "nodes"),
-    )
+        "nodes",
+    )
+    summed = lax.psum(half, "events")
     scaled = [value * scale_factor for value in summed]
     return (
         updated[None],

time: 245 us -> 189 us (0.77)
  waiting for transfers between devices: 128 us -> 87.1 us
  blocking collectives: 39.4 us -> 22 us
    psum x1, waiting for transfers between devices: 127 us -> 50.3 us  [shards(): lax.psum((edge_terms[0], edge_terms[1], edge_terms[2], edge_terms[3], nod...]
    psum x0 -> x1, waiting for transfers between devices: none -> 35.6 us  [shards(): summed = lax.psum(half, 'events')]
    psum x1, blocking collectives: 39.4 us -> 11.6 us  [shards(): lax.psum((edge_terms[0], edge_terms[1], edge_terms[2], edge_terms[3], nod...]
    psum x0 -> x1, blocking collectives: none -> 10.4 us  [shards(): summed = lax.psum(half, 'events')]
    unnamed x66 -> x70, local copies, waits for them, and re-layouts: 7.1 us -> 8.4 us
  transfers between devices with their start and end apart: 3 -> 4, of which waited for: 2 -> 3; matrix products, arithmetic and copies ran while one was open for 6% -> 9% of each run, Pallas kernels for 0% -> 0%
where the time goes in v1:
time: 189 us; the launch traced here: 187 us
  waiting for transfers between devices  87.1 us (46%)
  matrix products  28.1 us (15%)
  blocking collectives  22 us (12%)
  local copies, waits for them, and re-layouts  16.4 us (9%)
  between operations  14.4 us (8%)
  starting transfers between devices  12.4 us (7%)
  other arithmetic  6.59 us (3%)
    psum x1, waiting for transfers between devices, shards(): lax.psum((edge_terms[0], edge_terms[1], edge_terms[2], edge_terms[3], nod...  50.3 us
    psum x1, waiting for transfers between devices, shards(): summed = lax.psum(half, 'events')  35.6 us
    psum x1, blocking collectives, shards(): lax.psum((edge_terms[0], edge_terms[1], edge_terms[2], edge_terms[3], nod...  11.6 us
    psum x1, blocking collectives, shards(): summed = lax.psum(half, 'events')  10.4 us
    unnamed x70, local copies, waits for them, and re-layouts  8.4 us
    all_to_all x1, starting transfers between devices, shards(): lax.all_to_all(g_src.astype(jnp.bfloat16), 'nodes', split_axis=0, concat_...  7.04 us
    all_to_all x1, starting transfers between devices, shards(): lax.all_to_all(outgoing, 'nodes', split_axis=0, concat_axis=0, tiled=True)  5.35 us
    gather x3, local copies, waits for them, and re-layouts, gather_tiles(): picked = table.reshape(-1, tile, table.shape[-1])[blocks]  4.81 us
  transfers between devices with their start and end apart: 4, of which 3 were waited for; matrix products, arithmetic and copies ran while one was open for 9% of the time, Pallas kernels for 0%

profile of v1, /device:TPU:1, one launch (start us, length us, event | category | flops | bytes accessed | tf_op | source)
XLA Modules:
  0.0 187.0 jit_solution(9945788451820599952)
XLA Ops:
  8.1 1.7 gather_fusion
  9.8 1.3 convolution_convert_fusion.4
  11.1 5.4 %all-to-all-start = ((bf16[8,2,128,128]{3,2,1,0:T(8,128)(2,1)}), bf16[8,2,128,128]{3,2,1,0:T(8,128)(2,1)S(1)}, u32[]{:S(2)}, u32[]{:S(2)}) async-start(bf16[8,2,128,128]{3,2,1,0:T(8,128)(2,1)} %bitcast.6), calls=%async_computation | async-start | bytes 1048576 | tf_op jit(solution)/shard_map/all_to_all | solution.py:75
  20.8 1.2 fusion.25
  22.0 1.1 all-to-all-done
  24.4 1.4 multiply_convert_fusion.1
  28.0 1.2 convolution_convert_fusion.5
  30.0 1.3 multiply_convert_fusion
  33.0 1.1 convolution_convert_fusion.1
  34.1 2.5 %gather_fusion.2 = bf16[16,128,128]{2,1,0:T(8,128)(2,1)} fusion(bf16[16,128,128]{2,1,0:T(8,128)(2,1)} %bitcast.107, s32[1024]{0:T(1024)S(1)} %pad_clamp_fusion), kind=kCustom, calls=%fused_computation.2 | custom fusion | bytes 1048640 | tf_op jit(solution)/shard_map/gather | solution.py:20
  36.5 2.3 %convert_reduce_fusion.2 = (f32[128]{0:T(128)}, bf16[16,128,128]{2,1,0:T(8,128)(2,1)S(1)}) fusion(bf16[16]{0:T(256)(128)(2,1)S(1)} %reshape.170, bf16[16,128,128]{2,1,0:T(8,128)(2,1)} %gather_fusion.2, s32[16,128]{1,0:T(8,128)S(1)} %bitcast.111), kind=kOutput, calls=%fused_computation.39 | convolution fusion | flops 68419456 | bytes 1057312 | tf_op jit(solution)/shard_map/ten,tnd->ted/dot_general | solution.py:21
  43.4 1.1 convolution_convert_fusion
  46.5 7.0 %all-to-all-start.1 = ((bf16[8,2,128,128]{3,2,1,0:T(8,128)(2,1)}), bf16[8,2,128,128]{3,2,1,0:T(8,128)(2,1)}, u32[]{:S(2)}, u32[]{:S(2)}) async-start(bf16[8,2,128,128]{3,2,1,0:T(8,128)(2,1)} %bitcast.104), calls=%async_computation.1 | async-start | bytes 1048576 | tf_op jit(solution)/shard_map/all_to_all | solution.py:133
  53.6 1.5 fusion.19
  55.1 2.2 %fusion.15 = f32[16,128,128]{2,0,1:T(8,128)} fusion(f32[16,128,128]{2,1,0:T(8,128)S(1)} %fusion.19, s32[16]{0:T(128)S(1)} %copy-done.19), kind=kOutput, calls=%fused_computation.35 | convolution fusion | flops 50331904 | bytes 2097216 | tf_op jit(solution)/shard_map/tb,tnd->bnd/dot_general | solution.py:36
  58.0 11.6 %all-reduce = (f32[128]{0:T(128)S(1)}, f32[128]{0:T(128)S(1)}, f32[128]{0:T(128)S(1)}, f32[128]{0:T(128)S(1)}) all-reduce(f32[128]{0:T(128)S(1)} %copy-done.28, f32[128]{0:T(128)S(1)} %copy-done.26, f32[128]{0:T(128)S(1)} %copy-done.25, f32[128]{0:T(128)S(1)} %copy-done.22), channel_id=1, replica_groups=mesh['events'=4,'nodes'=8] {'nodes'}, use_global_device_ids=true, to_apply=%region_3.4 | all-reduce | flops 512 | bytes 4096 | tf_op jit(solution)/shard_map/psum | solution.py:158
  69.6 10.4 %all-reduce.2 = (f32[128]{0:T(128)S(1)}, f32[128]{0:T(128)S(1)}, f32[128]{0:T(128)S(1)}, f32[128]{0:T(128)}) all-reduce(f32[128]{0:T(128)S(1)} %get-tuple-element.10, f32[128]{0:T(128)S(1)} %get-tuple-element.11, f32[128]{0:T(128)S(1)} %get-tuple-element.12, ...), channel_id=1, replica_groups=mesh['events'=4,'nodes'=8] {'events'}, use_global_device_ids=true, to_apply=%region_4.5 | all-reduce | flops 512 | bytes 4096 | tf_op jit(solution)/shard_map/psum | solution.py:171
  83.7 1.6 copy.36
  86.5 50.3 %all-reduce.7.cloned.1.call-done = (f32[384,128]{1,0:T(8,128)}, f32[128,128]{1,0:T(8,128)}, f32[256,128]{1,0:T(8,128)}, f32[128,128]{1,0:T(8,128)}) async-done(((f32[384,128]{1,0:T(8,128)}, f32[128,128]{1,0:T(8,128)}, f32[256,128]{1,0:T(8,128)}, f32[128,128]{1,0:T(8,128)}), (f32[384,128]{1,0:T(8,128)}, f32[128,128]{1,0:T(8,128)}, f32[256,128]{1,0:T(8,128)}, ...) | async-done | bytes 458768 | tf_op jit(solution)/shard_map/psum | solution.py:158
  136.8 1.8 fusion.18
  138.6 1.2 fusion.13
  140.2 1.1 fusion.10
  141.3 35.6 %all-reduce.9.cloned.1.call-done = (f32[384,128]{1,0:T(8,128)}, f32[128,128]{1,0:T(8,128)}, f32[256,128]{1,0:T(8,128)}, f32[128,128]{1,0:T(8,128)}) async-done(((f32[384,128]{1,0:T(8,128)}, f32[128,128]{1,0:T(8,128)}, f32[256,128]{1,0:T(8,128)}, f32[128,128]{1,0:T(8,128)}), (f32[384,128]{1,0:T(8,128)}, f32[128,128]{1,0:T(8,128)}, f32[256,128]{1,0:T(8,128)}, ...) | async-done | bytes 458768 | tf_op jit(solution)/shard_map/psum | solution.py:171
  176.9 1.7 broadcast_multiply_fusion
  (114 shorter events, 25.1 us)
Async XLA Ops:
  7.2 16.6 %copy-start = (bf16[1,1,8,2,128,128]{5,4,3,2,1,0:T(8,128)(2,1)S(1)}, bf16[1,1,8,2,128,128]{5,4,3,2,1,0:T(8,128)(2,1)}, u32[]{:S(2)}) copy-start(bf16[1,1,8,2,128,128]{5,4,3,2,1,0:T(8,128)(2,1)} %param.17) | copy-start | bytes 1572868
  8.1 1.7 copy-start.15
  11.1 6.2 %copy-start.1 = (bf16[1,2048,128]{2,1,0:T(8,128)(2,1)S(1)}, bf16[1,2048,128]{2,1,0:T(8,128)(2,1)}, u32[]{:S(2)}) copy-start(bf16[1,2048,128]{2,1,0:T(8,128)(2,1)} %param.16) | copy-start | bytes 1572868
  11.1 12.1 %all-to-all-start = ((bf16[8,2,128,128]{3,2,1,0:T(8,128)(2,1)}), bf16[8,2,128,128]{3,2,1,0:T(8,128)(2,1)S(1)}, u32[]{:S(2)}, u32[]{:S(2)}) async-start(bf16[8,2,128,128]{3,2,1,0:T(8,128)(2,1)} %bitcast.6), calls=%async_computation | async-start | bytes 1048576 | tf_op jit(solution)/shard_map/all_to_all | solution.py:75
  18.7 1.3 copy-start.2
  19.8 8.1 %copy-start.18 = (s32[16]{0:T(128)}, s32[16]{0:T(128)S(1)}, u32[]{:S(2)}) copy-start(s32[16]{0:T(128)S(1)} %eq.32) | copy-start | bytes 196
  20.8 2.4 %copy-start.8 = (bf16[384,128]{1,0:T(8,128)(2,1)S(1)}, bf16[384,128]{1,0:T(8,128)(2,1)}, u32[]{:S(2)}) copy-start(bf16[384,128]{1,0:T(8,128)(2,1)} %param.23) | copy-start | bytes 294916
  24.4 1.5 copy-start.29
  25.8 1.1 copy-start.6
  28.0 1.4 copy-start.5
  30.0 1.3 copy-start.16
  38.8 1.0 copy-start.7
  38.8 2.0 %copy-start.33 = (f32[2048,128]{1,0:T(8,128)S(1)}, f32[2048,128]{1,0:T(8,128)}, u32[]{:S(2)}) copy-start(f32[2048,128]{1,0:T(8,128)} %get-tuple-element.27) | copy-start | bytes 3145732
  42.5 0.9 copy-start.9
  44.5 1.0 copy-start.3
  46.5 90.3 %all-to-all-start.1 = ((bf16[8,2,128,128]{3,2,1,0:T(8,128)(2,1)}), bf16[8,2,128,128]{3,2,1,0:T(8,128)(2,1)}, u32[]{:S(2)}, u32[]{:S(2)}) async-start(bf16[8,2,128,128]{3,2,1,0:T(8,128)(2,1)} %bitcast.104), calls=%async_computation.1 | async-start | bytes 1048576 | tf_op jit(solution)/shard_map/all_to_all | solution.py:133
  53.6 83.2 %all-reduce.7.cloned.1.call-start = ((), (), s32[]{:S(2)}) async-start(), calls=%async_computation.2 | async-start | bytes 917504 | tf_op jit(solution)/shard_map/psum | solution.py:158
  53.6 1.5 copy-start.19
  55.1 2.2 %copy-start.28 = (f32[128]{0:T(128)S(1)}, f32[128]{0:T(128)}, u32[]{:S(2)}) copy-start(f32[128]{0:T(128)} %get-tuple-element.30) | copy-start | bytes 1540
  80.5 1.4 copy-start.4
  81.9 95.0 %all-reduce.9.cloned.1.call-start = ((), (), s32[]{:S(2)}) async-start(), calls=%async_computation.3 | async-start | bytes 917504 | tf_op jit(solution)/shard_map/psum | solution.py:171
  136.8 1.8 copy-start.21
  176.9 1.7 copy-start.11
  178.6 0.9 copy-start.14
  (14 other events, 9.9 us)
Sparse Core Ops, SparseCore 0:
  82.0 54.7 all-reduce.6
  139.4 37.4 all-reduce.8
